TPU v7x, 32 devices: a whole 2x2x4 slice. The times are simulated.
32 devices in a mesh: energy: 8 (over z, x), slab: 4 (over y, core).
Axes of the slice: x: 2, y: 2, z: 4, core: 2. Of those that a mesh axis runs over, the one named last changes fastest.
Arguments:
- g_rows: bfloat16 [2, 1536, 4, 64, 384], P(None, 'energy', 'slab'), may hold values from -3 to 3
- injection: bfloat16 [4, 384, 384], P('slab'), may hold values from -0.3125 to 0.3125
- neighbour_ids: int32 [4, 256, 4], P('slab', 'energy'), may hold values from 0 to 5
- coupling: float32 [4, 256, 4], P('slab', 'energy'), may hold values from -4 to 4
Outputs:
- self_energy: bfloat16 [2, 1536, 4, 4096], P(None, 'energy', 'slab')
Inputs may be any that keep to these rules, and one draw needn't show every extreme that they name: `neighbour_ids`: an entry v names the neighbour pair in slab offset v // 2 - 1 and at place v % 2 within the tile's group of 2 consecutive tiles.
All inputs are finite; a program needn't handle non-finite values.
Results may differ from a plain program's by a relative error of at most 0.007.
Values may be sent and summed in bfloat16 or wider, within the bound.
A program may use at most 128 MiB of HBM per device.

v0:
```python
import jax
import jax.numpy as jnp
from jax import lax
from jax.sharding import PartitionSpec as P

TILE_ENTRIES = 16
GROUP = 2


radix_size = 32
spectral_mode = lax.Precision.HIGH


def with_halo(x, sides, width):
    for axis, dim in sides:
        size, length = (lax.axis_size(axis), x.shape[dim])
        up = [(i, (i + 1) % size) for i in range(size - 1)]
        down = [(j, i) for i, j in up]
        last = lax.slice_in_dim(x, length - width, length, axis=dim)
        initial = lax.slice_in_dim(x, 0, width, axis=dim)
        before = lax.ppermute(last, axis, up)
        after = lax.ppermute(initial, axis, down)
        x = jnp.concatenate([before, x, after], axis=dim)
    return x


def contract(pattern, first_operand, second_operand):
    return jnp.einsum(pattern, first_operand, second_operand, precision=spectral_mode)


def angle_tables(rows, cols, period):
    row_index = lax.iota(jnp.int32, rows)[:, None]
    col_index = lax.iota(jnp.int32, cols)[None, :]
    phase = (row_index * col_index % period).astype(jnp.float32) * (2.0 * jnp.pi / period)
    return (jnp.cos(phase), jnp.sin(phase))


def make_tables(energies):
    length_total = 2 * energies
    second_len = length_total // radix_size
    cos_first, sin_first = angle_tables(radix_size, radix_size // 2, radix_size)
    cos_twist, sin_twist = angle_tables(radix_size, second_len, length_total)
    cos_second, sin_second = angle_tables(second_len, second_len, second_len)
    return (cos_first, sin_first, cos_twist, sin_twist, cos_second, sin_second)


def spectrum(real_in, imag_in, tables):
    cos_first, sin_first, cos_twist, sin_twist, cos_second, sin_second = tables
    half_radix = cos_first.shape[1]
    second_len = cos_second.shape[0]
    columns = real_in.shape[1]
    real_grid = real_in.reshape(half_radix, second_len, columns)
    imag_grid = imag_in.reshape(half_radix, second_len, columns)
    real_one = contract("kn,nqc->kqc", cos_first, real_grid) + contract(
        "kn,nqc->kqc", sin_first, imag_grid
    )
    imag_one = contract("kn,nqc->kqc", cos_first, imag_grid) - contract(
        "kn,nqc->kqc", sin_first, real_grid
    )
    twist_cos = cos_twist[:, :, None]
    twist_sin = sin_twist[:, :, None]
    real_two = real_one * twist_cos + imag_one * twist_sin
    imag_two = imag_one * twist_cos - real_one * twist_sin
    real_out = contract("kn,pnc->pkc", cos_second, real_two) + contract(
        "kn,pnc->pkc", sin_second, imag_two
    )
    imag_out = contract("kn,pnc->pkc", cos_second, imag_two) - contract(
        "kn,pnc->pkc", sin_second, real_two
    )
    return (real_out, imag_out)


def inverse_spectrum(real_in, imag_in, tables):
    cos_first, sin_first, cos_twist, sin_twist, cos_second, sin_second = tables
    second_len = cos_second.shape[0]
    columns = real_in.shape[2]
    real_one = contract("kn,pkc->pnc", cos_second, real_in) - contract(
        "kn,pkc->pnc", sin_second, imag_in
    )
    imag_one = contract("kn,pkc->pnc", cos_second, imag_in) + contract(
        "kn,pkc->pnc", sin_second, real_in
    )
    twist_cos = cos_twist[:, :, None]
    twist_sin = sin_twist[:, :, None]
    real_two = real_one * twist_cos - imag_one * twist_sin
    imag_two = imag_one * twist_cos + real_one * twist_sin
    real_out = contract("kn,kqc->nqc", cos_first, real_two) - contract(
        "kn,kqc->nqc", sin_first, imag_two
    )
    imag_out = contract("kn,kqc->nqc", cos_first, imag_two) + contract(
        "kn,kqc->nqc", sin_first, real_two
    )
    inverse_norm = 1.0 / (radix_size * second_len)
    return (
        real_out.reshape(-1, columns) * inverse_norm,
        imag_out.reshape(-1, columns) * inverse_norm,
    )


def lesser_block(green_part, inject):
    scattered = jnp.einsum(
        "xerb,bc->xerc", green_part, inject, preferred_element_type=jnp.float32
    ).astype(jnp.bfloat16)
    real_part = jnp.einsum(
        "erc,esc->ers", scattered[0], green_part[0], preferred_element_type=jnp.float32
    ) + jnp.einsum("erc,esc->ers", scattered[1], green_part[1], preferred_element_type=jnp.float32)
    imag_part = jnp.einsum(
        "erc,esc->ers", scattered[1], green_part[0], preferred_element_type=jnp.float32
    ) - jnp.einsum("erc,esc->ers", scattered[0], green_part[1], preferred_element_type=jnp.float32)
    stacked = jnp.stack([real_part, imag_part]).astype(jnp.bfloat16)
    return stacked.reshape(2, stacked.shape[1], -1)


def local(g_rows, injection, neighbour_ids, coupling):
    green_rows = g_rows[:, :, 0]
    inject = injection[0]
    devices = lax.axis_size("energy")
    half_count = green_rows.shape[1] // 2
    pieces = []
    for h in range(2):
        lesser_half = lesser_block(green_rows[:, h * half_count : (h + 1) * half_count], inject)
        pieces.append(
            lax.all_to_all(lesser_half, "energy", split_axis=2, concat_axis=1, tiled=True)
        )
    width_local = pieces[0].shape[2]
    joined = jnp.stack(
        [piece.reshape(2, devices, half_count, width_local) for piece in pieces], axis=2
    )
    gathered = joined.reshape(2, devices * 2 * half_count, width_local)
    energies = gathered.shape[1]
    width_local = gathered.shape[2]
    beside_all = with_halo(gathered[None], (("slab", 0),), 1)
    tiles_local = neighbour_ids.shape[1]
    groups_local = tiles_local // GROUP
    candidates = lax.iota(jnp.int32, 3 * GROUP)
    matches = (neighbour_ids[0][:, :, None] == candidates[None, None, :]).astype(jnp.float32)
    weights = jnp.sum(matches * coupling[0][:, :, None], axis=1).reshape(
        groups_local, GROUP, 3, GROUP
    )
    nearby = beside_all.reshape(3, 2, energies, groups_local, GROUP, TILE_ENTRIES).astype(
        jnp.float32
    )
    interaction = jnp.einsum(
        "gpoq,oxegqc->xegpc", weights, nearby, precision=lax.Precision.HIGHEST
    ).reshape(2, energies, width_local)
    own_tiles = gathered.astype(jnp.float32)
    tables = make_tables(energies)
    real_spec, imag_spec = spectrum(
        jnp.concatenate([own_tiles[0], interaction[0]], axis=1),
        jnp.concatenate([own_tiles[1], interaction[1]], axis=1),
        tables,
    )
    lesser_real = real_spec[:, :, :width_local]
    lesser_imag = imag_spec[:, :, :width_local]
    inter_real = real_spec[:, :, width_local:]
    inter_imag = imag_spec[:, :, width_local:]
    product_real = lesser_real * inter_real - lesser_imag * inter_imag
    product_imag = lesser_real * inter_imag + lesser_imag * inter_real
    conv_real, conv_imag = inverse_spectrum(product_real, product_imag, tables)
    factor = energies ** (-0.5)
    result = (jnp.stack([conv_real, conv_imag]) * factor).astype(jnp.bfloat16)
    returned = lax.all_to_all(result, "energy", split_axis=1, concat_axis=2, tiled=True)
    return returned[:, :, None, :]


def solution(mesh):
    in_specs = (
        P(None, "energy", "slab", None, None),
        P("slab", None, None),
        P("slab", "energy", None),
        P("slab", "energy", None),
    )
    out_specs = P(None, "energy", "slab", None)
    return jax.shard_map(local, mesh=mesh, in_specs=in_specs, out_specs=out_specs, check_vma=False)
```

profile of v0, /device:TPU:0, one launch (start us, length us, event | category | flops | bytes accessed | tf_op | source)
XLA Modules:
  0.0 624.1 jit_solution(6109393369721337467)
XLA Ops:
  1.0 11.1 %convolution_convert_fusion.1 = bf16[2,96,64,384]{3,2,1,0:T(8,128)(2,1)} fusion(bf16[1,384,384]{2,1,0:T(8,128)(2,1)S(1)} %copy-done, bf16[2,192,1,64,384]{4,3,2,1,0:T(8,128)(2,1)} %param.4), kind=kOutput, calls=%fused_computation.32 | convolution fusion | flops 3628597248 | bytes 28606464 | tf_op jit(solution)/shard_map/xerb,bc->xerc/dot_general | solution.py:101
  12.0 5.9 fusion.27
  17.9 5.9 fusion.28
  23.9 5.3 subtract_convert_fusion.1
  30.9 7.6 %add_convert_fusion.1 = bf16[96,64,64]{2,1,0:T(8,128)(2,1)} fusion(f32[96,64,64]{2,1,0:T(8,128)} %fusion.28, bf16[2,192,64,384]{3,2,1,0:T(8,128)(2,1)} %bitcast.171, bf16[2,96,64,384]{3,2,1,0:T(8,128)(2,1)} %convolution_convert_fusion.1), kind=kOutput, calls=%fused_computation.59 | convolution fusion | flops 302776320 | bytes 13369344 | tf_op jit(solution)/shard_map/erc,esc->ers/dot_general | solution.py:106
  41.9 18.1 %copy.233 = bf16[2,96,4096]{1,0,2:T(2,128)(2,1)} copy(bf16[2,96,4096]{1,2,0:T(8,128)(2,1)S(1)} %pad_maximum_fusion.11) | data formatting | bytes 3145728 | tf_op jit(solution)/shard_map/stack | solution.py:110
  60.0 7.4 %all-to-all-start = ((bf16[2,96,4096]{1,0,2:T(2,128)(2,1)}), bf16[2,96,4096]{1,0,2:T(2,128)(2,1)}, u32[]{:S(2)}, u32[]{:S(2)}) async-start(bf16[2,96,4096]{1,0,2:T(2,128)(2,1)} %copy.233), calls=%async_computation | async-start | bytes 4194304 | tf_op jit(solution)/shard_map/all_to_all | solution.py:123
  67.4 11.0 %convolution_convert_fusion = bf16[2,96,64,384]{3,2,1,0:T(8,128)(2,1)} fusion(bf16[1,384,384]{2,1,0:T(8,128)(2,1)S(1)} %copy-done, bf16[2,192,1,64,384]{4,3,2,1,0:T(8,128)(2,1)} %param.4), kind=kOutput, calls=%fused_computation.31 | convolution fusion | flops 3628597248 | bytes 28606464 | tf_op jit(solution)/shard_map/xerb,bc->xerc/dot_general | solution.py:101
  79.5 5.8 fusion.32
  85.2 6.3 %add_convert_fusion = bf16[96,64,64]{2,1,0:T(8,128)(2,1)} fusion(f32[96,64,64]{2,1,0:T(8,128)} %fusion.32, bf16[2,192,64,384]{3,2,1,0:T(8,128)(2,1)S(1)} %bitcast.180, bf16[2,96,64,384]{3,2,1,0:T(8,128)(2,1)} %convolution_convert_fusion), kind=kOutput, calls=%fused_computation.57 | convolution fusion | flops 302776320 | bytes 13369344 | tf_op jit(solution)/shard_map/erc,esc->ers/dot_general | solution.py:106
  94.3 5.6 fusion.31
  99.8 6.8 %subtract_convert_fusion = bf16[96,64,64]{2,1,0:T(8,128)(2,1)} fusion(f32[96,64,64]{2,1,0:T(8,128)S(1)} %fusion.31, bf16[2,192,64,384]{3,2,1,0:T(8,128)(2,1)} %bitcast.173, bf16[2,96,64,384]{3,2,1,0:T(8,128)(2,1)} %convolution_convert_fusion), kind=kOutput, calls=%fused_computation.56 | convolution fusion | flops 302776320 | bytes 11796480 | tf_op jit(solution)/shard_map/erc,esc->ers/dot_general | solution.py:107
  110.2 18.1 %copy.238 = bf16[2,96,4096]{1,0,2:T(2,128)(2,1)} copy(bf16[2,96,4096]{1,2,0:T(8,128)(2,1)S(1)} %pad_maximum_fusion.12) | data formatting | bytes 3145728 | tf_op jit(solution)/shard_map/stack | solution.py:110
  128.4 6.0 all-to-all-start.1
  134.4 6.0 copy.283
  140.4 41.7 %all-to-all-done.1 = bf16[2,96,4096]{1,0,2:T(2,128)(2,1)S(1)} async-done(((bf16[2,96,4096]{1,0,2:T(2,128)(2,1)}), bf16[2,96,4096]{1,0,2:T(2,128)(2,1)S(1)}, u32[]{:S(2)}, u32[]{:S(2)}) %all-to-all-start.1) | async-done | bytes 1572896 | tf_op jit(solution)/shard_map/all_to_all | solution.py:123
  185.6 5.1 fusion.187
  197.3 7.9 %copy.244 = bf16[2,8,2,96,512]{3,2,1,4,0:T(2,128)(2,1)} copy(bf16[2,8,2,96,512]{4,3,1,0,2:T(8,128)(2,1)S(1)} %get-tuple-element.16) | data formatting | bytes 6291456 | tf_op jit(solution)/shard_map/stack | solution.py:126
  205.2 12.6 %concatenate.32 = bf16[1,2,1536,16,2,16]{2,5,4,3,1,0:T(8,128)(2,1)} reshape(bf16[2,8,2,96,512]{3,2,1,4,0:T(2,128)(2,1)} %copy.244) | data formatting | bytes 6291456 | tf_op jit(solution)/shard_map/concatenate | solution.py:23
  217.8 7.1 %copy.247 = bf16[1,2,1536,16,2,16]{2,0,4,5,1,3:T(2,128)(2,1)} copy(bf16[1,2,1536,16,2,16]{2,5,4,3,1,0:T(8,128)(2,1)} %concatenate.32) | data formatting | bytes 6291456 | tf_op jit(solution)/shard_map/concatenate | solution.py:23
  233.2 6.0 copy.241
  243.2 4.7 copy.243
  247.8 6.9 %copy.246 = bf16[1,2,1536,16,2,16]{2,0,4,5,1,3:T(2,128)(2,1)} copy(bf16[1,2,1536,16,2,16]{2,5,4,3,1,0:T(8,128)(2,1)} %bitcast.186) | data formatting | bytes 6291456 | tf_op jit(solution)/shard_map/concatenate | solution.py:23
  254.8 4.6 copy.245
  259.4 6.8 %copy.248 = bf16[1,2,1536,16,2,16]{2,0,4,5,1,3:T(2,128)(2,1)S(1)} copy(bf16[1,2,1536,16,2,16]{2,5,4,3,1,0:T(8,128)(2,1)} %bitcast.187) | data formatting | bytes 6291456 | tf_op jit(solution)/shard_map/concatenate | solution.py:23
  266.3 41.8 %fusion.9 = f32[2,1536,16,2,16]{1,3,4,0,2:T(2,128)S(1)} fusion(bf16[1,2,1536,16,2,16]{2,0,4,5,1,3:T(2,128)(2,1)S(1)} %copy.248, bf16[1,2,1536,16,2,16]{2,0,4,5,1,3:T(2,128)(2,1)} %copy.247, bf16[1,2,1536,16,2,16]{2,0,4,5,1,3:T(2,128)(2,1)S(1)} %copy-done.7, f32[16,2,3,2,1,1]{1,0,3,2,5,4:T(8,128)S(1)} %bitcast.195), kind=kOutput, calls=%fused_computation.14 | convolution fusion | flops 141557760 | bytes 15729408 | tf_op jit(solution)/shard_map/gpoq,oxegqc->xegpc/dot_general | solution.py:143
  308.1 4.2 fusion.189
  314.5 5.1 concatenate.35
  319.7 5.2 copy.251
  324.9 8.5 %fusion.22 = f32[32,96,1024]{2,0,1:T(8,128)} fusion(f32[16,96,512]{2,0,1:T(8,128)} %copy.251, f32[16,96,512]{2,0,1:T(8,128)S(1)} %concatenate.30), kind=kOutput, calls=%fused_computation.36 | convolution fusion | flops 303569920 | bytes 18874368 | tf_op jit(solution)/shard_map/kn,nqc->kqc/dot_general | solution.py:28
  333.4 7.8 %fusion.21 = f32[32,96,1024]{2,0,1:T(8,128)} fusion(f32[16,96,512]{2,0,1:T(8,128)S(1)} %copy-done.5, f32[16,96,512]{2,0,1:T(8,128)S(1)} %concatenate.30), kind=kOutput, calls=%fused_computation.35 | convolution fusion | flops 303569920 | bytes 18874368 | tf_op jit(solution)/shard_map/kn,nqc->kqc/dot_general | solution.py:28
  348.5 9.0 %fusion.20 = f32[32,96,1024]{2,0,1:T(8,128)} fusion(f32[16,96,512]{2,0,1:T(8,128)S(1)} %copy.254, f32[16,96,512]{2,0,1:T(8,128)} %concatenate.37), kind=kOutput, calls=%fused_computation.34 | convolution fusion | flops 303569920 | bytes 18874368 | tf_op jit(solution)/shard_map/kn,nqc->kqc/dot_general | solution.py:28
  357.5 25.0 %multiply_add_fusion = (f32[32,96,1024]{2,0,1:T(8,128)}, f32[32,96,1024]{2,0,1:T(8,128)}) fusion(f32[32,96]{0,1:T(8,128)S(1)} %copy.256, f32[32,96]{0,1:T(8,128)S(1)} %copy.255, f32[32,96,1024]{2,0,1:T(8,128)} %fusion.21, f32[32,96,1024]{2,0,1:T(8,128)} %fusion.22, f32[32,96,1024]{2,0,1:T(8,128)} %fusion.20, f32[16,96,512]{2,0,1:T(8,128)S(1)} %copy.254, ...), kind=kOutput, calls=%fused_computation.4 | convolution fusion | flops 328735744 | bytes 69230592 | tf_op jit(solution)/shard_map/kn,nqc->kqc/dot_general | solution.py:28
  382.4 21.7 %fusion.3 = f32[32,1024,96]{1,2,0:T(8,128)} fusion(f32[32,96,1024]{2,0,1:T(8,128)} %get-tuple-element.6), kind=kOutput, calls=%fused_computation.8 | convolution fusion | flops 1812022272 | bytes 25165824 | tf_op jit(solution)/shard_map/kn,pnc->pkc/dot_general | solution.py:28
  404.1 15.5 %fusion.1 = f32[32,1024,96]{1,2,0:T(8,128)} fusion(f32[32,96,1024]{2,0,1:T(8,128)S(1)} %copy-done.2), kind=kOutput, calls=%fused_computation.6 | convolution fusion | flops 1812022272 | bytes 25165824 | tf_op jit(solution)/shard_map/kn,pnc->pkc/dot_general | solution.py:28
  419.7 20.4 %add_bitcast_fusion = f32[32,96,1024]{2,1,0:T(8,128)} fusion(f32[32,1024,96]{1,2,0:T(8,128)} %fusion.3, f32[32,96,1024]{2,0,1:T(8,128)S(1)} %bitcast.168), kind=kOutput, calls=%fused_computation.2 | convolution fusion | flops 1815168000 | bytes 37748736 | tf_op jit(solution)/shard_map/kn,pnc->pkc/dot_general | solution.py:28
  440.0 20.5 %subtract_bitcast_fusion = f32[32,96,1024]{2,1,0:T(8,128)} fusion(f32[32,1024,96]{1,2,0:T(8,128)} %fusion.1, f32[32,96,1024]{2,0,1:T(8,128)S(1)} %bitcast.168), kind=kOutput, calls=%fused_computation.1 | convolution fusion | flops 1815168000 | bytes 37748736 | tf_op jit(solution)/shard_map/kn,pnc->pkc/dot_general | solution.py:28
  460.5 9.8 %multiply_subtract_fusion.1 = (f32[32,96,512]{2,1,0:T(8,128)S(1)}, f32[32,96,512]{2,1,0:T(8,128)S(1)}) fusion(f32[32,96,1024]{2,1,0:T(8,128)} %subtract_bitcast_fusion, f32[32,96,1024]{2,1,0:T(8,128)} %add_bitcast_fusion), kind=kLoop, calls=%fused_computation.22 | loop fusion | flops 9437184 | bytes 37748736 | tf_op jit(solution)/shard_map/sub | solution.py:157
  470.3 5.1 fusion.46
  475.4 5.0 fusion.50
  480.5 5.2 fusion.44
  485.7 13.6 %subtract_bitcast_fusion.1 = (f32[32,96,512]{2,1,0:T(8,128)}, f32[32,96,512]{2,1,0:T(8,128)}) fusion(f32[32,96]{1,0:T(8,128)S(1)} %get-tuple-element.17, f32[32,96]{1,0:T(8,128)S(1)} %get-tuple-element.18, f32[32,512,96]{1,2,0:T(8,128)} %fusion.50, f32[32,512,96]{1,2,0:T(8,128)} %fusion.44, f32[32,512,96]{1,2,0:T(8,128)} %fusion.46, ...), kind=kOutput, calls=%fused_computation.20 | convolution fusion | flops 918635520 | bytes 37773312 | tf_op jit(solution)/shard_map/kn,pkc->pnc/dot_general | solution.py:28
  499.2 8.6 %fusion.13 = f32[16,96,512]{2,0,1:T(8,128)S(1)} fusion(f32[32,96,512]{2,1,0:T(8,128)} %get-tuple-element.8), kind=kOutput, calls=%fused_computation.25 | convolution fusion | flops 151002112 | bytes 9437184 | tf_op jit(solution)/shard_map/kn,kqc->nqc/dot_general | solution.py:28
  507.8 5.2 fusion.11
  513.1 5.6 subtract_multiply_fusion
  520.7 5.6 add_multiply_fusion
  529.1 12.3 %copy.271 = bf16[2,1536,512]{2,0,1:T(2,128)(2,1)S(1)} copy(bf16[2,1536,512]{2,1,0:T(8,128)(2,1)S(1)} %fusion.10) | data formatting | bytes 6291456 | tf_op jit(solution)/shard_map/convert_element_type | solution.py:161
  541.5 76.5 %all_to_all.45 = bf16[2,1536,512]{2,0,1:T(2,128)(2,1)S(1)} all-to-all(bf16[2,1536,512]{2,0,1:T(2,128)(2,1)S(1)} %copy.271), channel_id=1, replica_groups=mesh['energy'=8,'slab'=4] {'energy'}, dimensions={1} | all-to-all | bytes 6291456 | tf_op jit(solution)/shard_map/all_to_all | solution.py:162
  (80 shorter events, 56.1 us)
Async XLA Ops:
  0.0 1.0 copy-start
  0.0 12.0 %copy-start.4 = (bf16[2,192,1,64,384]{4,3,2,1,0:T(8,128)(2,1)S(1)}, bf16[2,192,1,64,384]{4,3,2,1,0:T(8,128)(2,1)}, u32[]{:S(2)}) copy-start(bf16[2,192,1,64,384]{4,3,2,1,0:T(8,128)(2,1)} %param.4) | copy-start | bytes 56623108
  60.0 18.4 %slice-start.5 = ((s8[18874368]{0:T(1024)(128)(4,1)}), s8[2097152]{0:T(1024)(128)(4,1)S(1)}, s32[]{:S(2)}) async-start(s8[18874368]{0:T(1024)(128)(4,1)} %bitcast.177), calls=%async_computation.8 | async-start | bytes 4194304
  60.0 68.3 %all-to-all-start = ((bf16[2,96,4096]{1,0,2:T(2,128)(2,1)}), bf16[2,96,4096]{1,0,2:T(2,128)(2,1)}, u32[]{:S(2)}, u32[]{:S(2)}) async-start(bf16[2,96,4096]{1,0,2:T(2,128)(2,1)} %copy.233), calls=%async_computation | async-start | bytes 4194304 | tf_op jit(solution)/shard_map/all_to_all | solution.py:123
  67.4 11.0 %slice-start.6 = ((s8[18874368]{0:T(1024)(128)(4,1)}), s8[4194304]{0:T(1024)(128)(4,1)S(1)}, s32[]{:S(2)}) async-start(s8[18874368]{0:T(1024)(128)(4,1)} %bitcast.177), calls=%async_computation.9 | async-start | bytes 8388608
  67.4 11.0 %slice-start.7 = ((s8[18874368]{0:T(1024)(128)(4,1)}), s8[4194304]{0:T(1024)(128)(4,1)S(1)}, s32[]{:S(2)}) async-start(s8[18874368]{0:T(1024)(128)(4,1)} %bitcast.177), calls=%async_computation.10 | async-start | bytes 8388608
  67.4 11.0 %slice-start.8 = ((s8[18874368]{0:T(1024)(128)(4,1)}), s8[4194304]{0:T(1024)(128)(4,1)S(1)}, s32[]{:S(2)}) async-start(s8[18874368]{0:T(1024)(128)(4,1)} %bitcast.177), calls=%async_computation.11 | async-start | bytes 8388608
  67.4 12.0 %slice-start.9 = ((s8[18874368]{0:T(1024)(128)(4,1)}), s8[4194304]{0:T(1024)(128)(4,1)S(1)}, s32[]{:S(2)}) async-start(s8[18874368]{0:T(1024)(128)(4,1)} %bitcast.177), calls=%async_computation.12 | async-start | bytes 8388608
  128.4 53.7 %all-to-all-start.1 = ((bf16[2,96,4096]{1,0,2:T(2,128)(2,1)}), bf16[2,96,4096]{1,0,2:T(2,128)(2,1)S(1)}, u32[]{:S(2)}, u32[]{:S(2)}) async-start(bf16[2,96,4096]{1,0,2:T(2,128)(2,1)} %copy.238), calls=%async_computation.1 | async-start | bytes 4194304 | tf_op jit(solution)/shard_map/all_to_all | solution.py:123
  190.7 6.1 copy-start.8
  190.7 6.2 copy-start.9
  192.7 50.5 %collective-permute-start = (bf16[1,2,1536,512]{3,2,1,0:T(8,128)(2,1)}, bf16[1,2,1536,512]{3,2,1,0:T(8,128)(2,1)}, u32[]{:S(2)}, u32[]{:S(2)}) collective-permute-start(bf16[1,2,1536,512]{3,2,1,0:T(8,128)(2,1)} %bitcast.27), channel_id=1, source_target_pairs={{0,1},{1,2},{2,3},{4,5},{5,6},{6,7},{8,9},{9,10},{10,11},{12,13},{... | collective-permute-start | bytes 9437192 | tf_op jit(solution)/shard_map/ppermute | solution.py:21
  195.6 59.2 %collective-permute-start.1 = (bf16[1,2,1536,512]{3,2,1,0:T(8,128)(2,1)}, bf16[1,2,1536,512]{3,2,1,0:T(8,128)(2,1)}, u32[]{:S(2)}, u32[]{:S(2)}) collective-permute-start(bf16[1,2,1536,512]{3,2,1,0:T(8,128)(2,1)} %bitcast.27), channel_id=1, source_target_pairs={{1,0},{2,1},{3,2},{5,4},{6,5},{7,6},{9,8},{10,9},{11,10},{13,12},{... | collective-permute-start | bytes 9437192 | tf_op jit(solution)/shard_map/ppermute | solution.py:22
  205.2 19.7 %slice-start.10 = ((s8[6291456]{0:T(1024)(128)(4,1)}), s8[2097152]{0:T(1024)(128)(4,1)S(1)}, s32[]{:S(2)}) async-start(s8[6291456]{0:T(1024)(128)(4,1)} %bitcast.181), calls=%async_computation.13 | async-start | bytes 4194304
  217.8 7.1 %slice-start.11 = ((s8[6291456]{0:T(1024)(128)(4,1)}), s8[4194304]{0:T(1024)(128)(4,1)S(1)}, s32[]{:S(2)}) async-start(s8[6291456]{0:T(1024)(128)(4,1)} %bitcast.181), calls=%async_computation.14 | async-start | bytes 8388608
  259.4 6.9 %copy-start.7 = (bf16[1,2,1536,16,2,16]{2,0,4,5,1,3:T(2,128)(2,1)S(1)}, bf16[1,2,1536,16,2,16]{2,0,4,5,1,3:T(2,128)(2,1)}, u32[]{:S(2)}) copy-start(bf16[1,2,1536,16,2,16]{2,0,4,5,1,3:T(2,128)(2,1)} %copy.246) | copy-start | bytes 9437188
  324.9 8.5 %copy-start.5 = (f32[16,96,512]{2,0,1:T(8,128)S(1)}, f32[16,96,512]{2,0,1:T(8,128)}, u32[]{:S(2)}) copy-start(f32[16,96,512]{2,0,1:T(8,128)} %copy.251) | copy-start | bytes 9437188
  333.4 7.8 %copy-start.6 = (f32[1,1536,16,2,16]{1,3,4,0,2:T(2,128)S(1)}, f32[1,1536,16,2,16]{1,3,4,0,2:T(2,128)}, u32[]{:S(2)}) copy-start(f32[1,1536,16,2,16]{1,3,4,0,2:T(2,128)} %get-tuple-element.14) | copy-start | bytes 9437188
  382.4 21.7 %copy-start.2 = (f32[32,96,1024]{2,0,1:T(8,128)S(1)}, f32[32,96,1024]{2,0,1:T(8,128)}, u32[]{:S(2)}) copy-start(f32[32,96,1024]{2,0,1:T(8,128)} %get-tuple-element.6) | copy-start | bytes 37748740
  382.4 37.2 %slice-start = ((s8[12582912]{0:T(1024)(128)(4,1)}), s8[4194304]{0:T(1024)(128)(4,1)S(1)}, s32[]{:S(2)}) async-start(s8[12582912]{0:T(1024)(128)(4,1)} %bitcast.167), calls=%async_computation.3 | async-start | bytes 8388608
  382.4 37.2 %slice-start.1 = ((s8[12582912]{0:T(1024)(128)(4,1)}), s8[4194304]{0:T(1024)(128)(4,1)S(1)}, s32[]{:S(2)}) async-start(s8[12582912]{0:T(1024)(128)(4,1)} %bitcast.167), calls=%async_computation.4 | async-start | bytes 8388608
  404.1 15.5 %slice-start.2 = ((s8[12582912]{0:T(1024)(128)(4,1)}), s8[4194304]{0:T(1024)(128)(4,1)S(1)}, s32[]{:S(2)}) async-start(s8[12582912]{0:T(1024)(128)(4,1)} %bitcast.167), calls=%async_computation.5 | async-start | bytes 8388608
  499.2 8.6 %copy-start.3 = (f32[32,96,512]{2,1,0:T(8,128)S(1)}, f32[32,96,512]{2,1,0:T(8,128)}, u32[]{:S(2)}) copy-start(f32[32,96,512]{2,1,0:T(8,128)} %get-tuple-element.8) | copy-start | bytes 18874372
  499.2 13.8 %slice-start.3 = ((s8[6291456]{0:T(1024)(128)(4,1)}), s8[4194304]{0:T(1024)(128)(4,1)S(1)}, s32[]{:S(2)}) async-start(s8[6291456]{0:T(1024)(128)(4,1)} %bitcast.169), calls=%async_computation.6 | async-start | bytes 8388608
  507.8 5.2 slice-start.4
  618.5 5.2 copy-start.1
where the time goes:
time: 634 us; the launch traced here: 624 us
  matrix products  295 us (47%)
  local copies, waits for them, and re-layouts  176 us (28%)
  blocking collectives  76.5 us (12%)
  waiting for transfers between devices  41.7 us (7%)
  starting transfers between devices  17.6 us (3%)
  other arithmetic  17 us (3%)
    dot_general x16, matrix products, contract(): jnp.einsum(pattern, first_operand, second_operand, precision=spectral_mode)  182 us
    all_to_all x1, blocking collectives, local(): lax.all_to_all(result, 'energy', split_axis=1, concat_axis=2, tiled=True)  76.5 us
    dot_general x1, matrix products, local(): jnp.einsum('gpoq,oxegqc->xegpc', weights, nearby, precision=lax.Precision...  41.8 us
    all_to_all x2, waiting for transfers between devices, local(): lax.all_to_all(lesser_half, 'energy', split_axis=2, concat_axis=1, tiled=...  41.7 us
    another operation x2, local copies, waits for them, and re-layouts, lesser_block(): stacked = jnp.stack([real_part, imag_part]).astype(jnp.bfloat16)  36.2 us
    concatenate x4, local copies, waits for them, and re-layouts, with_halo(): x = jnp.concatenate([before, x, after], axis=dim)  33.4 us
    dot_general x2, matrix products, lesser_block(): jnp.einsum('xerb,bc->xerc', green_part, inject, preferred_element_type=jn...  22.1 us
    concatenate x3, local copies, waits for them, and re-layouts, local(): jnp.concatenate([own_tiles[0], interaction[0]], axis=1)  14.3 us
  transfers between devices with their start and end apart: 4, of which 1 were waited for; matrix products, arithmetic and copies ran while one was open for 20% of the time, Pallas kernels for 0%

commit v1 on v0

v1 whole, which is shorter than its diff:
```python
import functools

import jax
import jax.numpy as jnp
import numpy as np
from jax import lax
from jax.experimental import pallas as pl
from jax.experimental.pallas import tpu as pltpu
from jax.sharding import PartitionSpec as P

TILE_ENTRIES = 16
GROUP = 2
RADIX = 8
ROWS = 16
F32 = jnp.float32
BF16 = jnp.bfloat16
HALF_ROOT = 0.5**0.5


def dft_tables(energies):
    total = 2 * energies
    sub = total // RADIX
    j = np.arange(RADIX)[:, None, None]
    k = np.arange(sub)[None, :, None]
    n = np.arange(sub)[None, None, :]
    phase = ((RADIX * k + j) * n % total) * (2.0 * np.pi / total)
    c, s = np.cos(phase), np.sin(phase)
    forward = np.concatenate([np.concatenate([c, s], 2), np.concatenate([-s, c], 2)], 1)
    return forward.astype(np.float32).astype(BF16), forward.transpose(0, 2, 1).astype(np.float32).astype(BF16)


def pair_masks(window):
    side = np.arange(2)
    index = np.arange(window)
    r_side, r_part, r_col = [a.reshape(-1) for a in np.meshgrid(side, side, index, indexing="ij")]
    c_part, c_side, c_col = [a.reshape(-1) for a in np.meshgrid(side, side, index, indexing="ij")]
    same = (r_side[:, None] == c_side[None]) & (r_part[:, None] == c_part[None])
    perm = same & (r_col[:, None] == c_col[None])
    span = GROUP * TILE_ENTRIES
    near = (
        same
        & (r_col[:, None] // span == c_col[None] // span)
        & (r_col[:, None] % TILE_ENTRIES == c_col[None] % TILE_ENTRIES)
    )
    place = r_col[:, None] // TILE_ENTRIES % GROUP
    masks = [near & (place == q) for q in range(GROUP)] + [perm]
    return np.stack(masks).astype(np.float32)


def lesser_kernel(g_ref, inj_ref, out_ref):
    _, count, window, width = g_ref.shape
    g = g_ref[...]
    scattered = jnp.dot(
        g.reshape(2 * count * window, width), inj_ref[...], preferred_element_type=F32
    ).astype(BF16)
    scattered = scattered.reshape(2, count, window, width)
    left = jnp.concatenate([scattered[0], scattered[1]], axis=-1)
    right = jnp.concatenate(
        [jnp.concatenate([g[0], g[1]], axis=-1), jnp.concatenate([-g[1], g[0]], axis=-1)], axis=1
    )
    full = lax.dot_general(
        left, right, (((2,), (2,)), ((0,), (0,))), preferred_element_type=F32
    )
    out_ref[...] = jnp.swapaxes(full, 0, 1).astype(BF16)


def lesser_call(green, inject):
    _, count, window, width = green.shape
    block = 16
    return pl.pallas_call(
        lesser_kernel,
        grid=(count // block,),
        in_specs=[
            pl.BlockSpec((2, block, window, width), lambda i: (0, i, 0, 0)),
            pl.BlockSpec((width, width), lambda i: (0, 0)),
        ],
        out_specs=pl.BlockSpec((window, block, 2 * window), lambda i: (0, i, 0)),
        out_shape=jax.ShapeDtypeStruct((window, count, 2 * window), BF16),
        compiler_params=pltpu.CompilerParams(vmem_limit_bytes=48 * 2**20),
        cost_estimate=pl.CostEstimate(
            flops=2 * count * window * width * (2 * width + 4 * window),
            bytes_accessed=2 * 2 * count * window * (width + window),
            transcendentals=0,
        ),
        name="lesser",
    )(green, inject)


def mix(own, before, after, mask_ref, weight, z_ref, pair, pairs):
    half = own.shape[1] // 2
    total = None
    for o, x in enumerate((before, own, after)):
        m = mask_ref[0] * weight(o, 0) + mask_ref[1] * weight(o, 1)
        term = jnp.dot(x, m.astype(BF16), preferred_element_type=F32)
        total = term if total is None else total + term
    same = jnp.dot(own, mask_ref[2].astype(BF16), preferred_element_type=F32)
    for part in range(2):
        lanes = slice(part * half, (part + 1) * half)
        z_ref[part, :, pair * half : (pair + 1) * half] = same[:, lanes]
        z_ref[part, :, (pairs + pair) * half : (pairs + pair + 1) * half] = total[:, lanes]


def convolve(z_ref, fwd_ref, inv_ref, t_ref, v_ref, store, scale):
    _, energies, wide = z_ref.shape
    cols = wide // 2
    sub = 2 * energies // RADIX
    c = HALF_ROOT

    def split(i, carry):
        row = pl.multiple_of(i * ROWS, ROWS)
        for lane in range(0, wide, 256):
            lanes = pl.ds(lane, 256)
            re = [z_ref[0, pl.ds(b * sub + row, ROWS), lanes] for b in range(4)]
            im = [z_ref[1, pl.ds(b * sub + row, ROWS), lanes] for b in range(4)]

            def put(j, a, b):
                t_ref[j, pl.ds(row, ROWS), lanes] = a.astype(BF16)
                t_ref[j, pl.ds(sub + row, ROWS), lanes] = b.astype(BF16)

            def four(j, r, m):
                s0r, s0m, d0r, d0m = r[0] + r[2], m[0] + m[2], r[0] - r[2], m[0] - m[2]
                s1r, s1m, d1r, d1m = r[1] + r[3], m[1] + m[3], r[1] - r[3], m[1] - m[3]
                put(j, s0r + s1r, s0m + s1m)
                put(j + 2, d0r + d1m, d0m - d1r)
                put(j + 4, s0r - s1r, s0m - s1m)
                put(j + 6, d0r - d1m, d0m + d1r)

            four(0, re, im)
            tr = [re[0], (re[1] + im[1]) * c, im[2], (im[3] - re[3]) * c]
            tm = [im[0], (im[1] - re[1]) * c, -re[2], -(im[3] + re[3]) * c]
            four(1, tr, tm)
        return carry

    lax.fori_loop(0, sub // ROWS, split, 0)

    def spectral(j, carry):
        x = jnp.dot(fwd_ref[j], t_ref[j], preferred_element_type=F32)
        lr, li = x[:sub, :cols], x[sub:, :cols]
        ir, ii = x[:sub, cols:], x[sub:, cols:]
        p = jnp.concatenate([lr * ir - li * ii, lr * ii + li * ir], axis=0).astype(BF16)
        v_ref[j] = jnp.dot(inv_ref[j], p, preferred_element_type=F32)
        return carry

    lax.fori_loop(0, RADIX, spectral, 0)

    def gather(i, carry):
        row = pl.multiple_of(i * ROWS, ROWS)
        vr = [v_ref[j, pl.ds(row, ROWS), :] for j in range(RADIX)]
        vm = [v_ref[j, pl.ds(sub + row, ROWS), :] for j in range(RADIX)]

        def four(j):
            r, m = vr[j::2], vm[j::2]
            s0r, s0m, d0r, d0m = r[0] + r[2], m[0] + m[2], r[0] - r[2], m[0] - m[2]
            s1r, s1m, d1r, d1m = r[1] + r[3], m[1] + m[3], r[1] - r[3], m[1] - m[3]
            return (
                [s0r + s1r, d0r - d1m, s0r - s1r, d0r + d1m],
                [s0m + s1m, d0m + d1r, s0m - s1m, d0m - d1r],
            )

        er, em = four(0)
        ar, am = four(1)
        br = [ar[0], (ar[1] - am[1]) * c, -am[2], -(ar[3] + am[3]) * c]
        bm = [am[0], (ar[1] + am[1]) * c, ar[2], (ar[3] - am[3]) * c]
        for b in range(4):
            store(b * sub + row, (er[b] + br[b]) * scale, (em[b] + bm[b]) * scale)
        return carry

    lax.fori_loop(0, sub // ROWS, gather, 0)


def convolve_kernel(x_ref, lo_ref, hi_ref, w_ref, mask_ref, fwd_ref, inv_ref, out_ref, z_ref, t_ref, v_ref):
    devices, rows, count, lanes = x_ref.shape
    energies = devices * count
    pairs = rows // 2

    def both(ref, p):
        parts = [ref[:, 2 * p + a].reshape(energies, lanes) for a in range(2)]
        return jnp.concatenate(parts, axis=1)

    for p in range(pairs):
        mix(
            both(x_ref, p),
            both(lo_ref, p),
            both(hi_ref, p),
            mask_ref,
            lambda o, q: w_ref[p, pl.ds(o * 2 + q, 1), :],
            z_ref,
            p,
            pairs,
        )

    def store(row, real, imag):
        dest = row // count
        inside = pl.multiple_of(row % count, ROWS)
        out_ref[dest, 0, pl.ds(inside, ROWS), :] = real.astype(BF16)
        out_ref[dest, 1, pl.ds(inside, ROWS), :] = imag.astype(BF16)

    scale = energies**-0.5 / (2 * energies)
    convolve(z_ref, fwd_ref, inv_ref, t_ref, v_ref, store, scale)


def convolve_call(x, lo, hi, w, masks, fwd, inv):
    devices, rows, count, lanes = x.shape
    energies = devices * count
    cols = rows * lanes // 2
    sub = 2 * energies // RADIX
    vmem = pl.BlockSpec(memory_space=pltpu.VMEM)
    return pl.pallas_call(
        convolve_kernel,
        in_specs=[vmem] * 7,
        out_specs=vmem,
        out_shape=jax.ShapeDtypeStruct((devices, 2, count, cols), BF16),
        scratch_shapes=[
            pltpu.VMEM((2, energies, 2 * cols), F32),
            pltpu.VMEM((RADIX, 2 * sub, 2 * cols), BF16),
            pltpu.VMEM((RADIX, 2 * sub, cols), F32),
        ],
        compiler_params=pltpu.CompilerParams(vmem_limit_bytes=60 * 2**20),
        cost_estimate=pl.CostEstimate(
            flops=2 * RADIX * 4 * sub * sub * 3 * cols, bytes_accessed=24 * 2**20, transcendentals=0
        ),
        name="convolve",
    )(x, lo, hi, w, masks, fwd, inv)


def pair_weights(neighbour_ids, coupling, window):
    tiles = neighbour_ids.shape[0]
    candidates = lax.iota(jnp.int32, 3 * GROUP)
    matches = (neighbour_ids[:, :, None] == candidates).astype(F32)
    weights = jnp.sum(matches * coupling[:, :, None], axis=1)
    per_pair = 2 * window // TILE_ENTRIES
    weights = weights.reshape(tiles // per_pair, per_pair, 3 * GROUP).transpose(0, 2, 1)
    lanes = jnp.repeat(weights, TILE_ENTRIES, axis=2)
    lanes = jnp.concatenate([lanes, lanes], axis=2)
    return jnp.pad(lanes, ((0, 0), (0, 2), (0, 0)))


def local(g_rows, injection, neighbour_ids, coupling):
    green = g_rows[:, :, 0]
    devices = lax.axis_size("energy")
    slabs = lax.axis_size("slab")
    window = green.shape[2]
    count = green.shape[1]
    energies = devices * count
    rows = window // devices
    lesser = lesser_call(green, injection[0]).reshape(devices, rows, count, 2 * window)
    weights = pair_weights(neighbour_ids[0], coupling[0], window)
    masks = jnp.asarray(pair_masks(window))
    fwd, inv = (jnp.asarray(t) for t in dft_tables(energies))
    chunks = max(1, rows // 4)
    step = rows // chunks
    up = [(i, i + 1) for i in range(slabs - 1)]
    down = [(i + 1, i) for i in range(slabs - 1)]
    results = []
    for c in range(chunks):
        x = lax.all_to_all(lesser[:, c * step : (c + 1) * step], "energy", 0, 0, tiled=True)
        lo = lax.ppermute(x, "slab", up)
        hi = lax.ppermute(x, "slab", down)
        w = weights[c * step // 2 : (c + 1) * step // 2]
        y = convolve_call(x, lo, hi, w, masks, fwd, inv)
        results.append(lax.all_to_all(y, "energy", 0, 0, tiled=True))
    out = jnp.stack(results, axis=1)
    out = out.transpose(2, 3, 0, 1, 4).reshape(2, count, 1, window * window)
    return out


def solution(mesh):
    in_specs = (
        P(None, "energy", "slab", None, None),
        P("slab", None, None),
        P("slab", "energy", None),
        P("slab", "energy", None),
    )
    out_specs = P(None, "energy", "slab", None)
    return jax.shard_map(local, mesh=mesh, in_specs=in_specs, out_specs=out_specs, check_vma=False)
```

time: 634 us -> 221 us (0.35)
  the two profiles are of different devices: /device:TPU:0 before, /device:TPU:30 now
where the time goes in v1:
time: 221 us; the launch traced here: 219 us
  Pallas kernels  82.4 us (37%)
  blocking collectives  65.5 us (30%)
  waiting for transfers between devices  36.5 us (17%)
  starting transfers between devices  22 us (10%)
  local copies, waits for them, and re-layouts  11.7 us (5%)
    pallas_call x2, Pallas kernels, convolve_call(): pl.pallas_call(convolve_kernel, in_specs=[vmem] * 7, out_specs=vmem, out_...  56 us
    all_to_all x1, blocking collectives, local(): lax.all_to_all(lesser[:, c * step:(c + 1) * step], 'energy', 0, 0, tiled=...  40.4 us
    ppermute x2, waiting for transfers between devices, local(): hi = lax.ppermute(x, 'slab', down)  28.8 us
    pallas_call x1, Pallas kernels, lesser_call(): pl.pallas_call(lesser_kernel, grid=(count // block,), in_specs=[pl.BlockS...  26.5 us
    all_to_all x1, blocking collectives, local(): results.append(lax.all_to_all(y, 'energy', 0, 0, tiled=True))  25.2 us
    ppermute x2, waiting for transfers between devices, local(): lo = lax.ppermute(x, 'slab', up)  7.77 us
    all_to_all x1, starting transfers between devices, local(): lax.all_to_all(lesser[:, c * step:(c + 1) * step], 'energy', 0, 0, tiled=...  6.13 us
    ppermute x2, starting transfers between devices, local(): lo = lax.ppermute(x, 'slab', up)  6.07 us
  transfers between devices with their start and end apart: 6, of which 4 were waited for; matrix products, arithmetic and copies ran while one was open for 0% of the time, Pallas kernels for 26%

profile of v1, /device:TPU:30, one launch (start us, length us, event | category | flops | bytes accessed | tf_op | source)
XLA Modules:
  0.0 218.6 jit_solution(1260870739998346614)
XLA Ops:
  0.0 0.0 copy-start
  0.0 1.0 copy-done
  1.0 26.5 %lesser.1 = bf16[64,192,128]{2,1,0:T(8,128)(2,1)S(1)} custom-call(bf16[2,192,64,384]{3,2,1,0:T(8,128)(2,1)} %bitcast.24, bf16[384,384]{1,0:T(8,128)(2,1)S(1)} %bitcast.18), custom_call_target="tpu_custom_call" | custom-call | flops 9663676416 | bytes 22020096 | tf_op jit(solution)/shard_map/lesser/pallas_call | solution.py:70
  27.4 1.4 fusion
  28.8 40.4 %all_to_all.20.x_ref = bf16[8,4,192,128]{3,2,1,0:T(8,128)(2,1)S(1)} all-to-all(bf16[8,4,192,128]{3,2,1,0:T(8,128)(2,1)S(1)} %get-tuple-element.6), channel_id=1, replica_groups=mesh['energy'=8,'slab'=4] {'energy'}, dimensions={0} | all-to-all | bytes 3145728 | tf_op jit(solution)/shard_map/all_to_all | solution.py:256
  69.2 0.0 copy-start.2
  69.2 0.0 copy-start.3
  69.2 0.0 copy-start.4
  69.2 6.1 %all-to-all-start = ((bf16[8,4,192,128]{3,2,1,0:T(8,128)(2,1)}), bf16[8,4,192,128]{3,2,1,0:T(8,128)(2,1)S(1)}, u32[]{:S(2)}, u32[]{:S(2)}) async-start(bf16[8,4,192,128]{3,2,1,0:T(8,128)(2,1)} %get-tuple-element.5), calls=%async_computation | async-start | bytes 3145728 | tf_op jit(solution)/shard_map/all_to_all | solution.py:256
  75.4 1.9 collective-permute-start.3
  77.3 0.0 copy-done.2
  77.3 3.6 %collective-permute-start.2 = (bf16[8,4,192,128]{3,2,1,0:T(8,128)(2,1)S(1)}, bf16[8,4,192,128]{3,2,1,0:T(8,128)(2,1)}, u32[]{:S(2)}, u32[]{:S(2)}) collective-permute-start(bf16[8,4,192,128]{3,2,1,0:T(8,128)(2,1)S(1)} %all_to_all.20.x_ref), channel_id=1, source_target_pairs={{0,1},{1,2},{2,3},{4,5},{5,6},{6,7},{8,9},{9,10},{10,11},{12,13},{... | collective-permute-start | bytes 4718600 | tf_op jit(solution)/shard_map/ppermute | solution.py:257
  80.9 0.0 copy-done.3
  80.9 0.0 copy-done.4
  80.9 0.1 reshape.15
  81.0 0.1 broadcast_in_dim.4
  81.1 0.1 reshape.16
  81.2 0.6 fusion.1
  81.8 13.4 %collective-permute-done.3.hi_ref = bf16[8,4,192,128]{3,2,1,0:T(8,128)(2,1)} collective-permute-done((bf16[8,4,192,128]{3,2,1,0:T(8,128)(2,1)S(1)}, bf16[8,4,192,128]{3,2,1,0:T(8,128)(2,1)}, u32[]{:S(2)}, u32[]{:S(2)}) %collective-permute-start.3) | collective-permute-done | bytes 1572896 | tf_op jit(solution)/shard_map/ppermute | solution.py:258
  95.2 3.9 %collective-permute-done.2.lo_ref = bf16[8,4,192,128]{3,2,1,0:T(8,128)(2,1)} collective-permute-done((bf16[8,4,192,128]{3,2,1,0:T(8,128)(2,1)S(1)}, bf16[8,4,192,128]{3,2,1,0:T(8,128)(2,1)}, u32[]{:S(2)}, u32[]{:S(2)}) %collective-permute-start.2) | collective-permute-done | bytes 1572896 | tf_op jit(solution)/shard_map/ppermute | solution.py:257
  99.1 28.0 %convolve.3 = bf16[8,2,192,256]{3,2,1,0:T(8,128)(2,1)} custom-call(bf16[8,4,192,128]{3,2,1,0:T(8,128)(2,1)} %copy-done.2, bf16[8,4,192,128]{3,2,1,0:T(8,128)(2,1)} %collective-permute-done.2.lo_ref, bf16[8,4,192,128]{3,2,1,0:T(8,128)(2,1)} %collective-permute-done.3.hi_ref, f32[2,8,256]{2,1,0:T(8,128)} %get-tuple-element.8.w_ref, ...), custom_call_target="tpu_custom_call" | custom-call | flops 7247757312 | bytes 25165824 | tf_op jit(solution)/shard_map/convolve/pallas_call | solution.py:208
  127.1 0.0 all-to-all-done.x_ref
  127.1 0.0 copy-start.1
  127.1 6.0 %all-to-all-start.3 = ((bf16[8,2,192,256]{3,2,1,0:T(8,128)(2,1)}), bf16[8,2,192,256]{3,2,1,0:T(8,128)(2,1)S(1)}, u32[]{:S(2)}, u32[]{:S(2)}) async-start(bf16[8,2,192,256]{3,2,1,0:T(8,128)(2,1)} %convolve.3), calls=%async_computation.3 | async-start | bytes 3145728 | tf_op jit(solution)/shard_map/all_to_all | solution.py:261
  133.1 1.9 collective-permute-start.1
  135.1 0.0 copy-done.1
  135.1 2.5 %collective-permute-start = (bf16[8,4,192,128]{3,2,1,0:T(8,128)(2,1)S(1)}, bf16[8,4,192,128]{3,2,1,0:T(8,128)(2,1)S(1)}, u32[]{:S(2)}, u32[]{:S(2)}) collective-permute-start(bf16[8,4,192,128]{3,2,1,0:T(8,128)(2,1)S(1)} %all-to-all-done.x_ref), channel_id=1, source_target_pairs={{0,1},{1,2},{2,3},{4,5},{5,6},{6,7},{8,9},{9,10},{10,11},{12,13},{... | collective-permute-start | bytes 4718600 | tf_op jit(solution)/shard_map/ppermute | solution.py:257
  137.6 15.4 %collective-permute-done.1.hi_ref = bf16[8,4,192,128]{3,2,1,0:T(8,128)(2,1)S(1)} collective-permute-done((bf16[8,4,192,128]{3,2,1,0:T(8,128)(2,1)S(1)}, bf16[8,4,192,128]{3,2,1,0:T(8,128)(2,1)S(1)}, u32[]{:S(2)}, u32[]{:S(2)}) %collective-permute-start.1) | collective-permute-done | bytes 1572896 | tf_op jit(solution)/shard_map/ppermute | solution.py:258
  153.0 0.0 copy-start.5
  153.0 3.8 %collective-permute-done.lo_ref = bf16[8,4,192,128]{3,2,1,0:T(8,128)(2,1)S(1)} collective-permute-done((bf16[8,4,192,128]{3,2,1,0:T(8,128)(2,1)S(1)}, bf16[8,4,192,128]{3,2,1,0:T(8,128)(2,1)S(1)}, u32[]{:S(2)}, u32[]{:S(2)}) %collective-permute-start) | collective-permute-done | bytes 1572896 | tf_op jit(solution)/shard_map/ppermute | solution.py:257
  156.8 0.0 copy-done.5
  156.8 0.0 copy-start.6
  156.8 1.2 copy-done.6
  158.0 28.0 %convolve.2 = bf16[8,2,192,256]{3,2,1,0:T(8,128)(2,1)} custom-call(bf16[8,4,192,128]{3,2,1,0:T(8,128)(2,1)} %copy-done.1, bf16[8,4,192,128]{3,2,1,0:T(8,128)(2,1)} %copy-done.6, bf16[8,4,192,128]{3,2,1,0:T(8,128)(2,1)} %copy-done.5, f32[2,8,256]{2,1,0:T(8,128)} %get-tuple-element.7.w_ref, f32[3,256,256]{2,1,0:T(8,128)} %constant.11.clone.mask_ref, ...), custom_call_target="tpu_custom_call" | custom-call | flops 7247757312 | bytes 25165824 | tf_op jit(solution)/shard_map/convolve/pallas_call | solution.py:208
  185.9 0.0 all-to-all-done.3
  185.9 25.2 %all_to_all.21 = bf16[8,2,192,256]{3,2,1,0:T(8,128)(2,1)S(1)} all-to-all(bf16[8,2,192,256]{3,2,1,0:T(8,128)(2,1)} %convolve.2), channel_id=1, replica_groups=mesh['energy'=8,'slab'=4] {'energy'}, dimensions={0} | all-to-all | bytes 3145728 | tf_op jit(solution)/shard_map/all_to_all | solution.py:261
  211.1 0.3 maximum_bitcast_fusion
  211.4 3.2 %copy.18 = bf16[2,192,8,2,256]{4,3,2,1,0:T(2,128)(2,1)S(1)} copy(bf16[2,192,8,2,256]{4,1,0,2,3:T(8,128)(2,1)S(1)} %maximum_bitcast_fusion) | data formatting | bytes 6291456 | tf_op jit(solution)/shard_map/transpose | solution.py:263
  214.6 4.0 %reshape.17 = bf16[2,192,1,4096]{3,1,0,2:T(8,128)(2,1)} reshape(bf16[2,192,8,2,256]{4,3,2,1,0:T(2,128)(2,1)S(1)} %copy.18) | data formatting | bytes 6291456 | tf_op jit(solution)/shard_map/reshape | solution.py:263
  (3 shorter events, 0.0 us)
Async XLA Ops:
  0.0 1.0 copy-start
  69.2 8.1 %copy-start.2 = (bf16[8,4,192,128]{3,2,1,0:T(8,128)(2,1)}, bf16[8,4,192,128]{3,2,1,0:T(8,128)(2,1)S(1)}, u32[]{:S(2)}) copy-start(bf16[8,4,192,128]{3,2,1,0:T(8,128)(2,1)S(1)} %all_to_all.20.x_ref) | copy-start | bytes 4718596
  69.2 11.6 %copy-start.3 = (f32[1,32,4]{1,2,0:T(4,128)S(1)}, f32[1,32,4]{1,2,0:T(4,128)}, u32[]{:S(2)}) copy-start(f32[1,32,4]{1,2,0:T(4,128)} %param.10) | copy-start | bytes 1540
  69.2 11.6 %copy-start.4 = (s32[1,32,4]{1,2,0:T(4,128)S(1)}, s32[1,32,4]{1,2,0:T(4,128)}, u32[]{:S(2)}) copy-start(s32[1,32,4]{1,2,0:T(4,128)} %param.9) | copy-start | bytes 1540
  69.2 57.9 %all-to-all-start = ((bf16[8,4,192,128]{3,2,1,0:T(8,128)(2,1)}), bf16[8,4,192,128]{3,2,1,0:T(8,128)(2,1)S(1)}, u32[]{:S(2)}, u32[]{:S(2)}) async-start(bf16[8,4,192,128]{3,2,1,0:T(8,128)(2,1)} %get-tuple-element.5), calls=%async_computation | async-start | bytes 3145728 | tf_op jit(solution)/shard_map/all_to_all | solution.py:256
  75.4 19.8 %collective-permute-start.3 = (bf16[8,4,192,128]{3,2,1,0:T(8,128)(2,1)S(1)}, bf16[8,4,192,128]{3,2,1,0:T(8,128)(2,1)}, u32[]{:S(2)}, u32[]{:S(2)}) collective-permute-start(bf16[8,4,192,128]{3,2,1,0:T(8,128)(2,1)S(1)} %all_to_all.20.x_ref), channel_id=1, source_target_pairs={{1,0},{2,1},{3,2},{5,4},{6,5},{7,6},{9,8},{10,9},{11,10},{13,12},{... | collective-permute-start | bytes 4718600 | tf_op jit(solution)/shard_map/ppermute | solution.py:258
  77.3 21.8 %collective-permute-start.2 = (bf16[8,4,192,128]{3,2,1,0:T(8,128)(2,1)S(1)}, bf16[8,4,192,128]{3,2,1,0:T(8,128)(2,1)}, u32[]{:S(2)}, u32[]{:S(2)}) collective-permute-start(bf16[8,4,192,128]{3,2,1,0:T(8,128)(2,1)S(1)} %all_to_all.20.x_ref), channel_id=1, source_target_pairs={{0,1},{1,2},{2,3},{4,5},{5,6},{6,7},{8,9},{9,10},{10,11},{12,13},{... | collective-permute-start | bytes 4718600 | tf_op jit(solution)/shard_map/ppermute | solution.py:257
  127.1 7.9 %copy-start.1 = (bf16[8,4,192,128]{3,2,1,0:T(8,128)(2,1)}, bf16[8,4,192,128]{3,2,1,0:T(8,128)(2,1)S(1)}, u32[]{:S(2)}) copy-start(bf16[8,4,192,128]{3,2,1,0:T(8,128)(2,1)S(1)} %all-to-all-done.x_ref) | copy-start | bytes 4718596
  127.1 58.8 %all-to-all-start.3 = ((bf16[8,2,192,256]{3,2,1,0:T(8,128)(2,1)}), bf16[8,2,192,256]{3,2,1,0:T(8,128)(2,1)S(1)}, u32[]{:S(2)}, u32[]{:S(2)}) async-start(bf16[8,2,192,256]{3,2,1,0:T(8,128)(2,1)} %convolve.3), calls=%async_computation.3 | async-start | bytes 3145728 | tf_op jit(solution)/shard_map/all_to_all | solution.py:261
  133.1 19.8 %collective-permute-start.1 = (bf16[8,4,192,128]{3,2,1,0:T(8,128)(2,1)S(1)}, bf16[8,4,192,128]{3,2,1,0:T(8,128)(2,1)S(1)}, u32[]{:S(2)}, u32[]{:S(2)}) collective-permute-start(bf16[8,4,192,128]{3,2,1,0:T(8,128)(2,1)S(1)} %all-to-all-done.x_ref), channel_id=1, source_target_pairs={{1,0},{2,1},{3,2},{5,4},{6,5},{7,6},{9,8},{10,9},{11,10},{13,12},{... | collective-permute-start | bytes 4718600 | tf_op jit(solution)/shard_map/ppermute | solution.py:258
  135.1 21.7 %collective-permute-start = (bf16[8,4,192,128]{3,2,1,0:T(8,128)(2,1)S(1)}, bf16[8,4,192,128]{3,2,1,0:T(8,128)(2,1)S(1)}, u32[]{:S(2)}, u32[]{:S(2)}) collective-permute-start(bf16[8,4,192,128]{3,2,1,0:T(8,128)(2,1)S(1)} %all-to-all-done.x_ref), channel_id=1, source_target_pairs={{0,1},{1,2},{2,3},{4,5},{5,6},{6,7},{8,9},{9,10},{10,11},{12,13},{... | collective-permute-start | bytes 4718600 | tf_op jit(solution)/shard_map/ppermute | solution.py:257
  153.0 3.8 %copy-start.5 = (bf16[8,4,192,128]{3,2,1,0:T(8,128)(2,1)}, bf16[8,4,192,128]{3,2,1,0:T(8,128)(2,1)S(1)}, u32[]{:S(2)}) copy-start(bf16[8,4,192,128]{3,2,1,0:T(8,128)(2,1)S(1)} %collective-permute-done.1.hi_ref) | copy-start | bytes 4718596
  156.8 1.2 copy-start.6

commit v2 on v1

v2 whole, which is shorter than its diff:
```python
import functools

import jax
import jax.numpy as jnp
import numpy as np
from jax import lax
from jax.experimental import pallas as pl
from jax.experimental.pallas import tpu as pltpu
from jax.sharding import PartitionSpec as P

TILE_ENTRIES = 16
GROUP = 2
RADIX = 8
ROWS = 16
F32 = jnp.float32
BF16 = jnp.bfloat16
HALF_ROOT = 0.5**0.5
MESH = pl.DeviceIdType.MESH


def dft_tables(energies):
    total = 2 * energies
    sub = total // RADIX
    j = np.arange(RADIX)[:, None, None]
    k = np.arange(sub)[None, :, None]
    n = np.arange(sub)[None, None, :]
    phase = ((RADIX * k + j) * n % total) * (2.0 * np.pi / total)
    c, s = np.cos(phase), np.sin(phase)
    forward = np.concatenate([np.concatenate([c, s], 2), np.concatenate([-s, c], 2)], 1)
    return forward.astype(np.float32).astype(BF16), forward.transpose(0, 2, 1).astype(np.float32).astype(BF16)


def pair_masks(window):
    side = np.arange(2)
    index = np.arange(window)
    r_side, r_part, r_col = [a.reshape(-1) for a in np.meshgrid(side, side, index, indexing="ij")]
    c_part, c_side, c_col = [a.reshape(-1) for a in np.meshgrid(side, side, index, indexing="ij")]
    same = (r_side[:, None] == c_side[None]) & (r_part[:, None] == c_part[None])
    perm = same & (r_col[:, None] == c_col[None])
    span = GROUP * TILE_ENTRIES
    near = (
        same
        & (r_col[:, None] // span == c_col[None] // span)
        & (r_col[:, None] % TILE_ENTRIES == c_col[None] % TILE_ENTRIES)
    )
    place = r_col[:, None] // TILE_ENTRIES % GROUP
    masks = [near & (place == q) for q in range(GROUP)] + [perm]
    return np.stack(masks).astype(np.float32)


def lesser_block(g, inject):
    _, count, window, width = g.shape
    scattered = jnp.dot(
        g.reshape(2 * count * window, width), inject, preferred_element_type=F32
    ).astype(BF16)
    scattered = scattered.reshape(2, count, window, width)
    left = jnp.concatenate([scattered[0], scattered[1]], axis=-1)
    right = jnp.concatenate(
        [jnp.concatenate([g[0], g[1]], axis=-1), jnp.concatenate([-g[1], g[0]], axis=-1)], axis=1
    )
    full = lax.dot_general(
        left, right, (((2,), (2,)), ((0,), (0,))), preferred_element_type=F32
    )
    return jnp.swapaxes(full, 0, 1).astype(BF16)


def mix(own, before, after, mask_ref, weight, z_ref):
    half = own.shape[1] // 2
    total = None
    for o, x in enumerate((before, own, after)):
        m = mask_ref[0] * weight(o, 0) + mask_ref[1] * weight(o, 1)
        term = jnp.dot(x, m.astype(BF16), preferred_element_type=F32)
        total = term if total is None else total + term
    same = jnp.dot(own, mask_ref[2].astype(BF16), preferred_element_type=F32)
    for part in range(2):
        lanes = slice(part * half, (part + 1) * half)
        z_ref[part, :, :half] = same[:, lanes]
        z_ref[part, :, half:] = total[:, lanes]


def split_pair(z_ref, t_ref, pair, pairs):
    _, energies, wide = z_ref.shape
    half = wide // 2
    sub = 2 * energies // RADIX
    c = HALF_ROOT

    def split(i, carry):
        row = pl.multiple_of(i * ROWS, ROWS)
        for part in range(2):
            lanes = slice(part * half, (part + 1) * half)
            to = part * pairs * half + pair * half
            to = slice(to, to + half)
            re = [z_ref[0, pl.ds(b * sub + row, ROWS), lanes] for b in range(4)]
            im = [z_ref[1, pl.ds(b * sub + row, ROWS), lanes] for b in range(4)]

            def put(j, a, b):
                t_ref[j, pl.ds(row, ROWS), to] = a.astype(BF16)
                t_ref[j, pl.ds(sub + row, ROWS), to] = b.astype(BF16)

            def four(j, r, m):
                s0r, s0m, d0r, d0m = r[0] + r[2], m[0] + m[2], r[0] - r[2], m[0] - m[2]
                s1r, s1m, d1r, d1m = r[1] + r[3], m[1] + m[3], r[1] - r[3], m[1] - m[3]
                put(j, s0r + s1r, s0m + s1m)
                put(j + 2, d0r + d1m, d0m - d1r)
                put(j + 4, s0r - s1r, s0m - s1m)
                put(j + 6, d0r - d1m, d0m + d1r)

            four(0, re, im)
            tr = [re[0], (re[1] + im[1]) * c, im[2], (im[3] - re[3]) * c]
            tm = [im[0], (im[1] - re[1]) * c, -re[2], -(im[3] + re[3]) * c]
            four(1, tr, tm)
        return carry

    lax.fori_loop(0, sub // ROWS, split, 0)

def convolve(t_ref, fwd_ref, inv_ref, v_ref, store, scale, hooks):
    _, double, wide = t_ref.shape
    cols = wide // 2
    sub = double // 2
    c = HALF_ROOT

    def spectral(j, carry):
        x = jnp.dot(fwd_ref[j], t_ref[j], preferred_element_type=F32)
        lr, li = x[:sub, :cols], x[sub:, :cols]
        ir, ii = x[:sub, cols:], x[sub:, cols:]
        p = jnp.concatenate([lr * ir - li * ii, lr * ii + li * ir], axis=0).astype(BF16)
        v_ref[j] = jnp.dot(inv_ref[j], p, preferred_element_type=F32)
        return carry

    stage = RADIX // max(1, len(hooks))
    for start in range(0, RADIX, stage):
        lax.fori_loop(start, start + stage, spectral, 0)
        if hooks:
            hooks[start // stage]()

    def gather(i, carry):
        row = pl.multiple_of(i * ROWS, ROWS)
        vr = [v_ref[j, pl.ds(row, ROWS), :] for j in range(RADIX)]
        vm = [v_ref[j, pl.ds(sub + row, ROWS), :] for j in range(RADIX)]

        def four(j):
            r, m = vr[j::2], vm[j::2]
            s0r, s0m, d0r, d0m = r[0] + r[2], m[0] + m[2], r[0] - r[2], m[0] - m[2]
            s1r, s1m, d1r, d1m = r[1] + r[3], m[1] + m[3], r[1] - r[3], m[1] - m[3]
            return (
                [s0r + s1r, d0r - d1m, s0r - s1r, d0r + d1m],
                [s0m + s1m, d0m + d1r, s0m - s1m, d0m - d1r],
            )

        er, em = four(0)
        ar, am = four(1)
        br = [ar[0], (ar[1] - am[1]) * c, -am[2], -(ar[3] + am[3]) * c]
        bm = [am[0], (ar[1] + am[1]) * c, ar[2], (ar[3] - am[3]) * c]
        for b in range(4):
            store(b * sub + row, (er[b] + br[b]) * scale, (em[b] + bm[b]) * scale)
        return carry

    lax.fori_loop(0, sub // ROWS, gather, 0)


def fused_kernel(
    g_ref, inj_ref, w_ref, mask_ref, fwd_hbm, inv_hbm, out_ref,
    g_buf, send, rx, lo, hi, y, fwd, inv, z, t, v,
    g_sem, tab_sem, own_sem, a_send, a_recv, up_send, up_recv, down_send, down_recv,
    ret_own, ret_send, ret_recv,
):
    chunks, devices, rows, count, lanes = rx.shape
    energies = devices * count
    pairs = rows // 2
    cols = rows * lanes // 2
    block = g_buf.shape[2]
    groups = a_send.shape[1]
    span = count // groups
    me = lax.axis_index("energy")
    slab = lax.axis_index("slab")
    slabs = lax.axis_size("slab")
    has_up = slab < slabs - 1
    has_down = slab > 0

    def g_copy(i):
        start = pl.multiple_of(i * block, block)
        return pltpu.make_async_copy(
            g_ref.at[:, pl.ds(start, block)], g_buf.at[i % 2], g_sem.at[i % 2]
        )

    g_copy(0).start()
    fwd_copy = pltpu.make_async_copy(fwd_hbm, fwd, tab_sem.at[0])
    inv_copy = pltpu.make_async_copy(inv_hbm, inv, tab_sem.at[1])

    barrier = pltpu.get_barrier_semaphore()

    def greet(k, carry):
        pl.semaphore_signal(
            barrier, inc=1, device_id=((me + k) % devices, slab), device_id_type=MESH
        )
        return carry

    lax.fori_loop(1, devices, greet, 0)

    @pl.when(has_up)
    def _():
        pl.semaphore_signal(barrier, inc=1, device_id=(me, slab + 1), device_id_type=MESH)

    @pl.when(has_down)
    def _():
        pl.semaphore_signal(barrier, inc=1, device_id=(me, slab - 1), device_id_type=MESH)

    peers = devices - 1 + jnp.where(has_up, 1, 0) + jnp.where(has_down, 1, 0)
    pl.semaphore_wait(barrier, peers)

    def when_range(g):
        return pl.ds(pl.multiple_of(g * span, ROWS), span)

    def tile_copy(c, g, source, target, peer):
        part = when_range(g)
        return pltpu.make_async_remote_copy(
            src_ref=send.at[target, c * rows : (c + 1) * rows, part],
            dst_ref=rx.at[c, source, :, part],
            send_sem=a_send.at[c, g, target],
            recv_sem=a_recv.at[c, g, source],
            device_id=(peer, slab),
            device_id_type=MESH,
        )

    def own_copy(c, g):
        part = when_range(g)
        return pltpu.make_async_copy(
            send.at[me, c * rows : (c + 1) * rows, part], rx.at[c, me, :, part], own_sem.at[c, g]
        )

    def send_group(c, g):
        def one(k, carry):
            to = (me + k) % devices
            tile_copy(c, g, me, to, to).start()
            return carry

        lax.fori_loop(1, devices, one, 0)
        own_copy(c, g).start()

    def halo_copy(c, g, up):
        part = when_range(g)
        return pltpu.make_async_remote_copy(
            src_ref=rx.at[c, :, :, part],
            dst_ref=(lo if up else hi).at[c, :, :, part],
            send_sem=(up_send if up else down_send).at[c, g],
            recv_sem=(up_recv if up else down_recv).at[c, g],
            device_id=(me, slab + 1 if up else slab - 1),
            device_id_type=MESH,
        )

    def forward_group(c, g):
        def one(k, carry):
            source = (me + devices - k) % devices
            tile_copy(c, g, source, source, source).wait_recv()
            return carry

        lax.fori_loop(1, devices, one, 0)
        own_copy(c, g).wait()

        @pl.when(has_up)
        def _():
            halo_copy(c, g, True).start()

        @pl.when(has_down)
        def _():
            halo_copy(c, g, False).start()

    def wait_halos(c):
        def one(g, carry):
            @pl.when(has_down)
            def _():
                halo_copy(c, g, True).wait_recv()

            @pl.when(has_up)
            def _():
                halo_copy(c, g, False).wait_recv()

            return carry

        lax.fori_loop(0, groups, one, 0)

    steps = span // block

    def lesser_group(g, carry):
        def step(b, inner):
            i = g * steps + b

            @pl.when(i + 1 < groups * steps)
            def _():
                g_copy(i + 1).start()

            g_copy(i).wait()
            result = lesser_block(g_buf[i % 2], inj_ref[...])
            start = pl.multiple_of(i * block, block)
            send[:, :, pl.ds(start, block), :] = result.reshape(
                devices, chunks * rows, block, lanes
            )
            return inner

        lax.fori_loop(0, steps, step, 0)
        send_group(0, g)

        @pl.when(g > 0)
        def _():
            forward_group(0, g - 1)

        return carry

    @pl.when(slab == 0)
    def _():
        lo[...] = jnp.zeros_like(lo)

    @pl.when(slab == slabs - 1)
    def _():
        hi[...] = jnp.zeros_like(hi)

    fwd_copy.start()
    inv_copy.start()
    lax.fori_loop(0, groups, lesser_group, 0)
    for c in range(1, chunks):
        lax.fori_loop(0, groups, lambda g, carry: (send_group(c, g), carry)[1], 0)
    forward_group(0, groups - 1)
    fwd_copy.wait()
    inv_copy.wait()

    def both(ref, c, p):
        parts = [ref[c, :, 2 * p + a].reshape(energies, lanes) for a in range(2)]
        return jnp.concatenate(parts, axis=1)

    def return_copy(c, source, target, peer):
        at = pl.multiple_of(source * (chunks * cols) + c * cols, 128)
        return pltpu.make_async_remote_copy(
            src_ref=y.at[c, target],
            dst_ref=out_ref.at[:, :, pl.ds(at, cols)],
            send_sem=ret_send.at[c, target],
            recv_sem=ret_recv.at[c, source],
            device_id=(peer, slab),
            device_id_type=MESH,
        )

    def return_own(c):
        at = pl.multiple_of(me * (chunks * cols) + c * cols, 128)
        return pltpu.make_async_copy(
            y.at[c, me], out_ref.at[:, :, pl.ds(at, cols)], ret_own.at[c]
        )

    scale = energies**-0.5 / (2 * energies)
    for c in range(chunks):
        wait_halos(c)
        for p in range(pairs):
            mix(
                both(rx, c, p),
                both(lo, c, p),
                both(hi, c, p),
                mask_ref,
                lambda o, q: w_ref[c * pairs + p, pl.ds(o * 2 + q, 1), :],
                z,
            )
            split_pair(z, t, p, pairs)

        def store(row, real, imag):
            dest = row // count
            inside = pl.multiple_of(row % count, ROWS)
            y[c, dest, 0, pl.ds(inside, ROWS), :] = real.astype(BF16)
            y[c, dest, 1, pl.ds(inside, ROWS), :] = imag.astype(BF16)

        hooks = []
        if c + 1 < chunks:
            hooks = [functools.partial(forward_group, c + 1, g) for g in range(groups)]
        convolve(t, fwd, inv, v, store, scale, hooks)

        def give(k, carry):
            to = (me + k) % devices
            return_copy(c, me, to, to).start()
            return carry

        lax.fori_loop(1, devices, give, 0)
        return_own(c).start()

    for c in range(chunks):
        return_own(c).wait()

        def finish(k, carry):
            peer = (me + k) % devices
            return_copy(c, peer, peer, peer).wait()
            return carry

        lax.fori_loop(1, devices, finish, 0)

        def drain(g, carry):
            def one(k, inner):
                to = (me + k) % devices
                tile_copy(c, g, me, to, to).wait_send()
                return inner

            lax.fori_loop(1, devices, one, 0)

            @pl.when(has_up)
            def _():
                halo_copy(c, g, True).wait_send()

            @pl.when(has_down)
            def _():
                halo_copy(c, g, False).wait_send()

            return carry

        lax.fori_loop(0, groups, drain, 0)


def fused_call(green, inject, weights, masks, fwd, inv, devices):
    _, count, window, width = green.shape
    energies = devices * count
    local_rows = window // devices
    chunks = max(1, local_rows // 4)
    rows = local_rows // chunks
    lanes = 2 * window
    cols = rows * lanes // 2
    sub = 2 * energies // RADIX
    groups = max(1, count // 48)
    vmem = pl.BlockSpec(memory_space=pltpu.VMEM)
    hbm = pl.BlockSpec(memory_space=pl.ANY)
    dma = pltpu.SemaphoreType.DMA
    slots = pltpu.VMEM((chunks, devices, rows, count, lanes), BF16)
    return pl.pallas_call(
        fused_kernel,
        in_specs=[hbm, vmem, vmem, vmem, hbm, hbm],
        out_specs=hbm,
        out_shape=jax.ShapeDtypeStruct((2, count, window * window), BF16),
        scratch_shapes=[
            pltpu.VMEM((2, 2, ROWS, window, width), BF16),
            pltpu.VMEM((devices, local_rows, count, lanes), BF16),
            slots,
            slots,
            slots,
            pltpu.VMEM((chunks, devices, 2, count, cols), BF16),
            pltpu.VMEM(fwd.shape, BF16),
            pltpu.VMEM(inv.shape, BF16),
            pltpu.VMEM((2, energies, 2 * lanes), F32),
            pltpu.VMEM((RADIX, 2 * sub, 2 * cols), BF16),
            pltpu.VMEM((RADIX, 2 * sub, cols), F32),
            dma((2,)),
            dma((2,)),
            dma((chunks, groups)),
            dma((chunks, groups, devices)),
            dma((chunks, groups, devices)),
            dma((chunks, groups)),
            dma((chunks, groups)),
            dma((chunks, groups)),
            dma((chunks, groups)),
            dma((chunks,)),
            dma((chunks, devices)),
            dma((chunks, devices)),
        ],
        compiler_params=pltpu.CompilerParams(
            vmem_limit_bytes=63 * 2**20, collective_id=0, has_side_effects=True
        ),
        cost_estimate=pl.CostEstimate(
            flops=2 * count * window * width * (2 * width + 4 * window)
            + 2 * RADIX * 4 * sub * sub * 3 * cols * chunks,
            bytes_accessed=48 * 2**20,
            transcendentals=0,
        ),
        name="fused",
    )(green, inject, weights, masks, fwd, inv)


def pair_weights(neighbour_ids, coupling, window):
    tiles = neighbour_ids.shape[0]
    candidates = lax.iota(jnp.int32, 3 * GROUP)
    matches = (neighbour_ids[:, :, None] == candidates).astype(F32)
    weights = jnp.sum(matches * coupling[:, :, None], axis=1)
    per_pair = 2 * window // TILE_ENTRIES
    weights = weights.reshape(tiles // per_pair, per_pair, 3 * GROUP).transpose(0, 2, 1)
    lanes = jnp.repeat(weights, TILE_ENTRIES, axis=2)
    lanes = jnp.concatenate([lanes, lanes], axis=2)
    return jnp.pad(lanes, ((0, 0), (0, 2), (0, 0)))


def local(g_rows, injection, neighbour_ids, coupling):
    green = g_rows[:, :, 0]
    devices = lax.axis_size("energy")
    window = green.shape[2]
    count = green.shape[1]
    weights = pair_weights(neighbour_ids[0], coupling[0], window)
    masks = jnp.asarray(pair_masks(window))
    fwd, inv = (jnp.asarray(t) for t in dft_tables(devices * count))
    out = fused_call(green, injection[0], weights, masks, fwd, inv, devices)
    return out.reshape(2, count, 1, window * window)


def solution(mesh):
    in_specs = (
        P(None, "energy", "slab", None, None),
        P("slab", None, None),
        P("slab", "energy", None),
        P("slab", "energy", None),
    )
    out_specs = P(None, "energy", "slab", None)
    return jax.shard_map(local, mesh=mesh, in_specs=in_specs, out_specs=out_specs, check_vma=False)
```

time: 221 us -> 162 us (0.73); the launches traced: 219 us -> 162 us
  Pallas kernels: 82.4 us -> 157 us
  blocking collectives: 65.5 us -> 0 us
  waiting for transfers between devices: 36.5 us -> 0 us
  starting transfers between devices: 22 us -> 0 us
  local copies, waits for them, and re-layouts: 11.7 us -> 4.17 us
    pallas_call x3 -> x1, Pallas kernels: 82.4 us -> 157 us  [fused_call(): pl.pallas_call(fused_kernel, in_specs=[hbm, vmem, vmem, vmem, hbm, hbm],...]
    all_to_all x2 -> x0, blocking collectives: 65.5 us -> none  [the longest x1 40.4 us: local(): lax.all_to_all(lesser[:, c * step:(c + 1) * step], 'energy', 0, 0, tiled=...]
    ppermute x4 -> x0, waiting for transfers between devices: 36.5 us -> none  [the longest x2 28.8 us: local(): hi = lax.ppermute(x, 'slab', down)]
    all_to_all x2 -> x0, starting transfers between devices: 12.1 us -> none  [the longest x1 6.13 us: local(): lax.all_to_all(lesser[:, c * step:(c + 1) * step], 'energy', 0, 0, tiled=...]
    ppermute x4 -> x0, starting transfers between devices: 9.89 us -> none  [the longest x2 6.07 us: local(): lo = lax.ppermute(x, 'slab', up)]
    reshape x1 -> x0, local copies, waits for them, and re-layouts: 3.98 us -> none  [local(): out = out.transpose(2, 3, 0, 1, 4).reshape(2, count, 1, window * window)]
    transpose x1 -> x0, local copies, waits for them, and re-layouts: 3.24 us -> none  [local(): out = out.transpose(2, 3, 0, 1, 4).reshape(2, count, 1, window * window)]
  transfers between devices with their start and end apart: 6 -> 0, of which waited for: 4 -> 0; matrix products, arithmetic and copies ran while one was open for 0% -> 0% of each run, Pallas kernels for 26% -> 0%
where the time goes in v2:
time: 162 us
  Pallas kernels  157 us (97%)
  local copies, waits for them, and re-layouts  4.17 us (3%)
    pallas_call x1, Pallas kernels, fused_call(): pl.pallas_call(fused_kernel, in_specs=[hbm, vmem, vmem, vmem, hbm, hbm],...  157 us
    unnamed x1, local copies, waits for them, and re-layouts  3.91 us

profile of v2, /device:TPU:30, one launch (start us, length us, event | category | flops | bytes accessed | tf_op | source)
XLA Modules:
  0.0 162.1 jit_solution(13995318427082571592)
XLA Ops:
  0.0 0.7 select_reduce_fusion
  0.7 0.1 reshape.11
  0.8 0.1 broadcast_in_dim.4
  0.9 0.1 reshape.12
  1.0 0.6 select_maximum_fusion.w_ref
  1.6 156.6 %fused.1 = bf16[2,192,4096]{2,1,0:T(8,128)(2,1)} custom-call(bf16[2,192,64,384]{3,2,1,0:T(8,128)(2,1)} %bitcast.18, bf16[384,384]{1,0:T(8,128)(2,1)} %bitcast.19, f32[4,8,256]{2,1,0:T(8,128)} %select_maximum_fusion.w_ref, f32[3,256,256]{2,1,0:T(8,128)} %constant.11.clone.mask_ref, bf16[8,768,768]{2,1,0:T(8,128)(2,1)} %constant.12.clone.fwd_hbm, ...), custom_call_target="tpu_custom_call" | custom-call | flops 24159191040 | bytes 50331648 | tf_op jit(solution)/shard_map/fused/pallas_call | solution.py:425
  158.2 3.9 %copy.20 = bf16[2,192,1,4096]{3,1,2,0:T(8,128)(2,1)} copy(bf16[2,192,1,4096]{3,1,2,0:T(8,128)(2,1)} %bitcast.14) | data formatting | bytes 6291456
  (1 shorter events, 0.0 us)

commit v3 on v2

--- a/solution.py
+++ b/solution.py
@@ -66,11 +66,12 @@
 
 def mix(own, before, after, mask_ref, weight, z_ref):
     half = own.shape[1] // 2
-    total = None
-    for o, x in enumerate((before, own, after)):
-        m = mask_ref[0] * weight(o, 0) + mask_ref[1] * weight(o, 1)
-        term = jnp.dot(x, m.astype(BF16), preferred_element_type=F32)
-        total = term if total is None else total + term
+    blocks = [mask_ref[0] * weight(o, 0) + mask_ref[1] * weight(o, 1) for o in range(3)]
+    total = jnp.dot(
+        jnp.concatenate([before, own, after], axis=1),
+        jnp.concatenate(blocks, axis=0).astype(BF16),
+        preferred_element_type=F32,
+    )
     same = jnp.dot(own, mask_ref[2].astype(BF16), preferred_element_type=F32)
     for part in range(2):
         lanes = slice(part * half, (part + 1) * half)
@@ -214,7 +215,7 @@
     def tile_copy(c, g, source, target, peer):
         part = when_range(g)
         return pltpu.make_async_remote_copy(
-            src_ref=send.at[target, c * rows : (c + 1) * rows, part],
+            src_ref=send.at[target, pl.ds(c * rows, rows), part],
             dst_ref=rx.at[c, source, :, part],
             send_sem=a_send.at[c, g, target],
             recv_sem=a_recv.at[c, g, source],
@@ -225,7 +226,7 @@
     def own_copy(c, g):
         part = when_range(g)
         return pltpu.make_async_copy(
-            send.at[me, c * rows : (c + 1) * rows, part], rx.at[c, me, :, part], own_sem.at[c, g]
+            send.at[me, pl.ds(c * rows, rows), part], rx.at[c, me, :, part], own_sem.at[c, g]
         )
 
     def send_group(c, g):
@@ -280,6 +281,7 @@
         lax.fori_loop(0, groups, one, 0)
 
     steps = span // block
+    early = min(2, chunks)
 
     def lesser_group(g, carry):
         def step(b, inner):
@@ -298,7 +300,8 @@
             return inner
 
         lax.fori_loop(0, steps, step, 0)
-        send_group(0, g)
+        for c in range(early):
+            send_group(c, g)
 
         @pl.when(g > 0)
         def _():
@@ -317,7 +320,7 @@
     fwd_copy.start()
     inv_copy.start()
     lax.fori_loop(0, groups, lesser_group, 0)
-    for c in range(1, chunks):
+    for c in range(early, chunks):
         lax.fori_loop(0, groups, lambda g, carry: (send_group(c, g), carry)[1], 0)
     forward_group(0, groups - 1)
     fwd_copy.wait()
@@ -345,7 +348,7 @@
         )
 
     scale = energies**-0.5 / (2 * energies)
-    for c in range(chunks):
+    def chunk(c, none):
         wait_halos(c)
         for p in range(pairs):
             mix(
@@ -364,9 +367,12 @@
             y[c, dest, 0, pl.ds(inside, ROWS), :] = real.astype(BF16)
             y[c, dest, 1, pl.ds(inside, ROWS), :] = imag.astype(BF16)
 
-        hooks = []
-        if c + 1 < chunks:
-            hooks = [functools.partial(forward_group, c + 1, g) for g in range(groups)]
+        def ahead(g):
+            @pl.when(c + 1 < chunks)
+            def _():
+                forward_group(c + 1, g)
+
+        hooks = [functools.partial(ahead, g) for g in range(groups)]
         convolve(t, fwd, inv, v, store, scale, hooks)
 
         def give(k, carry):
@@ -376,8 +382,11 @@
 
         lax.fori_loop(1, devices, give, 0)
         return_own(c).start()
-
-    for c in range(chunks):
+        return none
+
+    lax.fori_loop(0, chunks, chunk, 0)
+
+    def close(c, none):
         return_own(c).wait()
 
         def finish(k, carry):
@@ -406,13 +415,16 @@
             return carry
 
         lax.fori_loop(0, groups, drain, 0)
+        return none
+
+    lax.fori_loop(0, chunks, close, 0)
 
 
 def fused_call(green, inject, weights, masks, fwd, inv, devices):
     _, count, window, width = green.shape
     energies = devices * count
     local_rows = window // devices
-    chunks = max(1, local_rows // 4)
+    chunks = max(1, local_rows // 2)
     rows = local_rows // chunks
     lanes = 2 * window
     cols = rows * lanes // 2

time: 162 us -> 163 us (level)
  no operation moved by 1% of the time
where the time goes in v3:
time: 163 us
  Pallas kernels  157 us (96%)
  local copies, waits for them, and re-layouts  4.17 us (3%)
    pallas_call x1, Pallas kernels, fused_call(): pl.pallas_call(fused_kernel, in_specs=[hbm, vmem, vmem, vmem, hbm, hbm],...  157 us
    unnamed x1, local copies, waits for them, and re-layouts  3.91 us

profile of v3, /device:TPU:30, one launch (start us, length us, event | category | flops | bytes accessed | tf_op | source)
XLA Modules:
  0.0 162.5 jit_solution(7294953521089422990)
XLA Ops:
  0.0 0.7 select_reduce_fusion
  0.7 0.1 reshape.11
  0.8 0.1 broadcast_in_dim.4
  0.9 0.1 reshape.12
  1.0 0.6 select_maximum_fusion.w_ref
  1.6 157.0 %fused.1 = bf16[2,192,4096]{2,1,0:T(8,128)(2,1)} custom-call(bf16[2,192,64,384]{3,2,1,0:T(8,128)(2,1)} %bitcast.18, bf16[384,384]{1,0:T(8,128)(2,1)} %bitcast.19, f32[4,8,256]{2,1,0:T(8,128)} %select_maximum_fusion.w_ref, f32[3,256,256]{2,1,0:T(8,128)} %constant.11.clone.mask_ref, bf16[8,768,768]{2,1,0:T(8,128)(2,1)} %constant.12.clone.fwd_hbm, ...), custom_call_target="tpu_custom_call" | custom-call | flops 24159191040 | bytes 50331648 | tf_op jit(solution)/shard_map/fused/pallas_call | solution.py:437
  158.6 3.9 %copy.20 = bf16[2,192,1,4096]{3,1,2,0:T(8,128)(2,1)} copy(bf16[2,192,1,4096]{3,1,2,0:T(8,128)(2,1)} %bitcast.14) | data formatting | bytes 6291456
  (1 shorter events, 0.0 us)
